TPU v7x, 512 devices: a whole 4x4x16 slice. The times are simulated.
512 devices in a mesh: gx: 16 (over x, y_lo, core), gy: 32 (over z, y_hi).
Axes of the slice: x: 4, y: 4 (y_hi: 2, y_lo: 2; y = y_hi * 2 + y_lo), z: 16, core: 2. Of those that a mesh axis runs over, the one named last changes fastest.
Arguments:
- volume: bfloat16 [2, 64, 512, 2048], P(None, None, 'gy', 'gx'), may hold values from -6 to 6
- pupil_phase: float32 [16, 512, 2048], P(None, 'gy', 'gx'), may hold values from -3.140625 to 3.140625
Outputs:
- decorrelation: float32 [16, 512, 2048], P(None, 'gy', 'gx')
All inputs are finite; a program needn't handle non-finite values.
Results may differ from a plain program's by a relative error of at most 0.0075.
Values may be sent and summed in bfloat16 or wider, within the bound.
A program may use at most 64 MiB of HBM per device.

v0:
```python
import math

import jax
import jax.numpy as jnp
from jax import lax
from jax.sharding import PartitionSpec as P

R = 4
Z = 16
LOW = 128


def with_halo(block, sides, width):
    for axis, dim in sides:
        count = lax.axis_size(axis)
        forward = [(i, i + 1) for i in range(count - 1)]
        backward = [(target, source) for source, target in forward]
        low = lax.ppermute(
            lax.slice_in_dim(block, block.shape[dim] - width, None, axis=dim), axis, forward
        )
        high = lax.ppermute(lax.slice_in_dim(block, 0, width, axis=dim), axis, backward)
        block = jnp.concatenate([low, block, high], axis=dim)
    return block


def tables(length, direction):
    indices = jnp.arange(length, dtype=jnp.int32)
    angles = (indices[:, None] * indices[None, :] % length).astype(jnp.float32) * (
        2.0 * math.pi / length
    )
    return (
        jnp.cos(angles).astype(jnp.bfloat16),
        (direction * jnp.sin(angles)).astype(jnp.bfloat16),
    )


def twiddle(high_len, length, direction):
    row_index = jnp.arange(high_len, dtype=jnp.int32)
    col_index = jnp.arange(LOW, dtype=jnp.int32)
    angles = (row_index[:, None] * col_index[None, :] % length).astype(jnp.float32) * (
        2.0 * math.pi / length
    )
    return (jnp.cos(angles), direction * jnp.sin(angles))


def contract(fields, cosine, sine_table, pattern):
    first_term = jnp.einsum(pattern, fields, cosine, preferred_element_type=jnp.float32)
    second_term = jnp.einsum(pattern, fields, sine_table, preferred_element_type=jnp.float32)
    return (first_term[0] - second_term[1], first_term[1] + second_term[0])


def rotate(real_part, imag_part, cosine, sine_table, factor):
    rotated_real = (real_part * cosine - imag_part * sine_table) * factor
    rotated_imag = (imag_part * cosine + real_part * sine_table) * factor
    return jnp.stack([rotated_real, rotated_imag]).astype(jnp.bfloat16)


def transform_pass(fields, prefix, suffix, inverse):
    direction = 1.0 if inverse else -1.0
    dims = fields.shape
    position = fields.ndim - 1 - len(suffix)
    length = dims[position]
    high_len = length // LOW
    split_fields = fields.reshape(dims[:position] + (high_len, LOW) + dims[position + 1 :])
    trailing = (1,) * len(suffix)
    high_cos, high_sin = tables(high_len, direction)
    low_cos, low_sin = tables(LOW, direction)
    twist_cos, twist_sin = twiddle(high_len, length, direction)
    twist_cos = twist_cos.reshape((high_len, LOW) + trailing)
    twist_sin = twist_sin.reshape((high_len, LOW) + trailing)
    if inverse:
        real_part, imag_part = contract(
            split_fields,
            low_cos,
            low_sin,
            prefix + "km" + suffix + ",ml->" + prefix + "kl" + suffix,
        )
        middle = rotate(real_part, imag_part, twist_cos, twist_sin, 1.0 / LOW)
        real_part, imag_part = contract(
            middle, high_cos, high_sin, prefix + "kl" + suffix + ",kh->" + prefix + "hl" + suffix
        )
        factor = 1.0 / high_len
    else:
        real_part, imag_part = contract(
            split_fields,
            high_cos,
            high_sin,
            prefix + "hl" + suffix + ",hk->" + prefix + "kl" + suffix,
        )
        middle = rotate(real_part, imag_part, twist_cos, twist_sin, 1.0)
        real_part, imag_part = contract(
            middle, low_cos, low_sin, prefix + "kl" + suffix + ",lm->" + prefix + "km" + suffix
        )
        factor = 1.0
    result = jnp.stack([real_part * factor, imag_part * factor]).astype(jnp.bfloat16)
    return result.reshape(dims)


def apply_pupil(fields, phase):
    values = fields.astype(jnp.float32)
    cosine = jnp.cos(phase)
    sine_table = jnp.sin(phase)
    return jnp.stack(
        [values[0] * cosine - values[1] * sine_table, values[0] * sine_table + values[1] * cosine]
    ).astype(jnp.bfloat16)


def pair_terms(fields):
    values = fields.astype(jnp.float32)
    real_part = values[0]
    imag_part = values[1]
    cross_real = jnp.sum(real_part[:-1] * real_part[1:] + imag_part[:-1] * imag_part[1:], axis=0)
    cross_imag = jnp.sum(imag_part[:-1] * real_part[1:] - real_part[:-1] * imag_part[1:], axis=0)
    power = real_part * real_part + imag_part * imag_part
    energy = 0.5 * jnp.sum(power[:-1] + power[1:], axis=0)
    return jnp.stack([cross_real, cross_imag, energy])


def box_sum(padded):
    depth_sum = padded[:, :-2] + padded[:, 1:-1] + padded[:, 2:]
    lateral = depth_sum[:, :, :-2] + depth_sum[:, :, 1:-1] + depth_sum[:, :, 2:]
    return lateral[..., :-2] + lateral[..., 1:-1] + lateral[..., 2:]


def local(volume, pupil_phase):
    slice_phase = jnp.tile(pupil_phase, (R, 1, 1))[None]
    gathered = lax.all_to_all(volume, "gy", split_axis=1, concat_axis=2, tiled=True)
    phase_lines = lax.all_to_all(
        slice_phase.astype(jnp.bfloat16), "gy", split_axis=1, concat_axis=2, tiled=True
    ).astype(slice_phase.dtype)
    spectral = transform_pass(gathered, "cs", "x", False)
    pencil = lax.all_to_all(spectral, "gx", split_axis=2, concat_axis=3, tiled=True)
    phase_pencil = lax.all_to_all(
        phase_lines.astype(jnp.bfloat16), "gx", split_axis=2, concat_axis=3, tiled=True
    ).astype(phase_lines.dtype)
    pencil = transform_pass(pencil, "csy", "", False)
    pencil = apply_pupil(pencil, phase_pencil[0])
    pencil = transform_pass(pencil, "csy", "", True)
    spectral = lax.all_to_all(pencil, "gx", split_axis=3, concat_axis=2, tiled=True)
    spatial = transform_pass(spectral, "cs", "x", True)
    restored = lax.all_to_all(spatial, "gy", split_axis=2, concat_axis=1, tiled=True)
    fields = restored.reshape(2, R, Z, restored.shape[2], restored.shape[3])
    wide_fields = with_halo(fields, (("gx", 4), ("gy", 3)), 1)
    extended = pair_terms(wide_fields)
    padded = jnp.pad(extended, ((0, 0), (1, 1), (0, 0), (0, 0)))
    box_sums = box_sum(padded)
    magnitude = jnp.sqrt(box_sums[0] * box_sums[0] + box_sums[1] * box_sums[1])
    return 1.0 - magnitude / (box_sums[2] + 1e-06)


def solution(mesh):
    return jax.shard_map(
        local,
        mesh=mesh,
        in_specs=(P(None, None, "gy", "gx"), P(None, "gy", "gx")),
        out_specs=P(None, "gy", "gx"),
        check_vma=False,
    )
```

profile of v0, /device:TPU:1, one launch (start us, length us, event | category | flops | bytes accessed | tf_op | source)
XLA Modules:
  0.0 213.4 jit_solution(14925294717821225618)
XLA Ops:
  1.7 18.7 %all-to-all-start.2 = ((bf16[1,64,16,128]{3,2,0,1:T(8,128)(2,1)}), bf16[1,64,16,128]{3,2,0,1:T(8,128)(2,1)S(1)}, u32[]{:S(2)}, u32[]{:S(2)}) async-start(bf16[1,64,16,128]{3,2,0,1:T(8,128)(2,1)} %bitcast.31), calls=%async_computation.2 | async-start | bytes 524288 | tf_op jit(solution)/shard_map/all_to_all | solution.py:128
  20.3 1.9 copy.162
  22.2 18.8 %all-to-all-done.2 = bf16[1,64,16,128]{3,2,0,1:T(8,128)(2,1)S(1)} async-done(((bf16[1,64,16,128]{3,2,0,1:T(8,128)(2,1)}), bf16[1,64,16,128]{3,2,0,1:T(8,128)(2,1)S(1)}, u32[]{:S(2)}, u32[]{:S(2)}) %all-to-all-start.2) | async-done | bytes 262176 | tf_op jit(solution)/shard_map/all_to_all | solution.py:128
  41.0 5.2 %all-to-all-start = ((bf16[2,64,16,128]{3,2,0,1:T(8,128)(2,1)}), bf16[2,64,16,128]{3,2,0,1:T(8,128)(2,1)S(1)}, u32[]{:S(2)}, u32[]{:S(2)}) async-start(bf16[2,64,16,128]{3,2,0,1:T(8,128)(2,1)} %copy.162), calls=%async_computation | async-start | bytes 1048576 | tf_op jit(solution)/shard_map/all_to_all | solution.py:127
  47.6 29.5 %all-to-all-done = bf16[2,64,16,128]{3,2,0,1:T(8,128)(2,1)S(1)} async-done(((bf16[2,64,16,128]{3,2,0,1:T(8,128)(2,1)}), bf16[2,64,16,128]{3,2,0,1:T(8,128)(2,1)S(1)}, u32[]{:S(2)}, u32[]{:S(2)}) %all-to-all-start) | async-done | bytes 524320 | tf_op jit(solution)/shard_map/all_to_all | solution.py:127
  77.1 7.8 %all-to-all-start.3 = ((bf16[1,2,512,128]{3,1,0,2:T(2,128)(2,1)}), bf16[1,2,512,128]{3,1,0,2:T(2,128)(2,1)S(1)}, u32[]{:S(2)}, u32[]{:S(2)}) async-start(bf16[1,2,512,128]{3,1,0,2:T(2,128)(2,1)} %copy.180), calls=%async_computation.3 | async-start | bytes 524288 | tf_op jit(solution)/shard_map/all_to_all | solution.py:133
  88.6 1.5 pad_maximum_fusion.2
  90.1 2.2 %all-to-all-done.3 = bf16[1,2,512,128]{3,1,0,2:T(2,128)(2,1)S(1)} async-done(((bf16[1,2,512,128]{3,1,0,2:T(2,128)(2,1)}), bf16[1,2,512,128]{3,1,0,2:T(2,128)(2,1)S(1)}, u32[]{:S(2)}, u32[]{:S(2)}) %all-to-all-start.3) | async-done | bytes 262176 | tf_op jit(solution)/shard_map/all_to_all | solution.py:133
  92.3 3.8 %all-to-all-start.1 = ((bf16[2,2,512,128]{3,1,0,2:T(2,128)(2,1)}), bf16[2,2,512,128]{3,1,0,2:T(2,128)(2,1)S(1)}, u32[]{:S(2)}, u32[]{:S(2)}) async-start(bf16[2,2,512,128]{3,1,0,2:T(2,128)(2,1)} %pad_maximum_fusion.2), calls=%async_computation.1 | async-start | bytes 1048576 | tf_op jit(solution)/shard_map/all_to_all | solution.py:132
  96.2 1.8 convert_sine_fusion
  98.6 7.1 %all-to-all-done.1 = bf16[2,2,512,128]{3,1,0,2:T(2,128)(2,1)S(1)} async-done(((bf16[2,2,512,128]{3,1,0,2:T(2,128)(2,1)}), bf16[2,2,512,128]{3,1,0,2:T(2,128)(2,1)S(1)}, u32[]{:S(2)}, u32[]{:S(2)}) %all-to-all-start.1) | async-done | bytes 524320 | tf_op jit(solution)/shard_map/all_to_all | solution.py:132
  110.1 3.7 %convert_reduce_fusion = (bf16[2,32,2048]{2,1,0:T(8,128)(2,1)S(1)}, bf16[2,32,2048]{2,1,0:T(8,128)(2,1)S(1)}) fusion(f32[1,2,32,2048]{3,0,2,1:T(1,128)S(1)} %bitcast.159, f32[1,2,32,2048]{3,0,2,1:T(1,128)S(1)} %bitcast.160, f32[2,2,32,2048]{3,0,2,1:T(2,128)S(1)} %maximum_convert_fusion.1), kind=kLoop, calls=%fused_computation.71 | loop fusion | flops 1048576 | bytes 2621440 | tf_op jit(solution)/shard_map/convert.14
  116.3 1.5 copy.186
  117.8 2.7 %reshape.235 = bf16[16,2,8192]{2,1,0:T(2,128)(2,1)} reshape(bf16[2048,2,2,32]{3,2,1,0:T(2,128)(2,1)S(1)} %bitcast.149) | data formatting | bytes 1048576
  120.4 4.9 %all-to-all-start.4 = ((bf16[16,2,8192]{2,1,0:T(2,128)(2,1)}), bf16[16,2,8192]{2,1,0:T(2,128)(2,1)S(1)}, u32[]{:S(2)}, u32[]{:S(2)}) async-start(bf16[16,2,8192]{2,1,0:T(2,128)(2,1)} %reshape.235), calls=%async_computation.4 | async-start | bytes 1048576 | tf_op jit(solution)/shard_map/all_to_all | solution.py:139
  125.5 9.5 %all-to-all-done.4 = bf16[16,2,8192]{2,1,0:T(2,128)(2,1)S(1)} async-done(((bf16[16,2,8192]{2,1,0:T(2,128)(2,1)}), bf16[16,2,8192]{2,1,0:T(2,128)(2,1)S(1)}, u32[]{:S(2)}, u32[]{:S(2)}) %all-to-all-start.4) | async-done | bytes 524320 | tf_op jit(solution)/shard_map/all_to_all | solution.py:139
  136.1 2.7 %copy.187 = bf16[2,2,32,16,128]{4,2,3,1,0:T(8,128)(2,1)S(1)} copy(bf16[2,2,32,16,128]{2,1,0,4,3:T(2,128)(2,1)S(1)} %bitcast.150) | data formatting | bytes 1048576 | tf_op jit(solution)/shard_map/all_to_all | solution.py:139
  143.7 35.7 %all_to_all.87 = bf16[2,2,512,128]{3,1,0,2:T(2,128)(2,1)S(1)} all-to-all(bf16[2,2,512,128]{3,1,0,2:T(2,128)(2,1)S(1)} %copy.193), channel_id=1, replica_groups=mesh['gx'=16,'gy'=32] {'gy'}, dimensions={2} | all-to-all | bytes 1048576 | tf_op jit(solution)/shard_map/all_to_all | solution.py:141
  179.8 5.6 %collective-permute-start = (bf16[2,4,16,16,1]{4,3,2,1,0:T(8,128)(2,1)S(1)}, bf16[2,4,16,16,1]{4,3,2,1,0:T(8,128)(2,1)S(1)}, u32[]{:S(2)}, u32[]{:S(2)}) collective-permute-start(bf16[2,4,16,16,1]{4,3,2,1,0:T(8,128)(2,1)S(1)} %get-tuple-element.27), channel_id=1, source_target_pairs={{0,32},{32,64},{64,96},{96,128},{128,160},{160,192},{192,224},{224... | collective-permute-start | bytes 12296 | tf_op jit(solution)/shard_map/ppermute | solution.py:18
  185.3 1.9 collective-permute-start.1
  187.3 11.1 %collective-permute-done = bf16[2,4,16,16,1]{4,3,2,1,0:T(8,128)(2,1)S(1)} collective-permute-done((bf16[2,4,16,16,1]{4,3,2,1,0:T(8,128)(2,1)S(1)}, bf16[2,4,16,16,1]{4,3,2,1,0:T(8,128)(2,1)S(1)}, u32[]{:S(2)}, u32[]{:S(2)}) %collective-permute-start) | collective-permute-done | bytes 4128 | tf_op jit(solution)/shard_map/ppermute | solution.py:18
  199.2 3.2 %collective-permute-start.2 = (bf16[2,4,16,1,130]{4,3,2,1,0:T(2,128)(2,1)S(1)}, bf16[2,4,16,1,130]{4,3,2,1,0:T(2,128)(2,1)S(1)}, u32[]{:S(2)}, u32[]{:S(2)}) collective-permute-start(bf16[2,4,16,1,130]{4,3,2,1,0:T(2,128)(2,1)S(1)} %get-tuple-element.25), channel_id=1, source_target_pairs={{0,1},{1,2},{2,3},{3,4},{4,5},{5,6},{6,7},{7,8},{8,9},{9,10},{10,1... | collective-permute-start | bytes 99848 | tf_op jit(solution)/shard_map/ppermute | solution.py:18
  204.3 5.3 %collective-permute-done.3 = bf16[2,4,16,1,130]{4,3,2,1,0:T(2,128)(2,1)S(1)} collective-permute-done((bf16[2,4,16,1,130]{4,3,2,1,0:T(2,128)(2,1)S(1)}, bf16[2,4,16,1,130]{4,3,2,1,0:T(2,128)(2,1)S(1)}, u32[]{:S(2)}, u32[]{:S(2)}) %collective-permute-start.3) | collective-permute-done | bytes 33312 | tf_op jit(solution)/shard_map/ppermute | solution.py:21
  209.6 1.6 maximum_convert_fusion
  (75 shorter events, 25.4 us)
Async XLA Ops:
  1.7 39.4 %all-to-all-start.2 = ((bf16[1,64,16,128]{3,2,0,1:T(8,128)(2,1)}), bf16[1,64,16,128]{3,2,0,1:T(8,128)(2,1)S(1)}, u32[]{:S(2)}, u32[]{:S(2)}) async-start(bf16[1,64,16,128]{3,2,0,1:T(8,128)(2,1)} %bitcast.31), calls=%async_computation.2 | async-start | bytes 524288 | tf_op jit(solution)/shard_map/all_to_all | solution.py:128
  41.0 36.0 %all-to-all-start = ((bf16[2,64,16,128]{3,2,0,1:T(8,128)(2,1)}), bf16[2,64,16,128]{3,2,0,1:T(8,128)(2,1)S(1)}, u32[]{:S(2)}, u32[]{:S(2)}) async-start(bf16[2,64,16,128]{3,2,0,1:T(8,128)(2,1)} %copy.162), calls=%async_computation | async-start | bytes 1048576 | tf_op jit(solution)/shard_map/all_to_all | solution.py:127
  77.1 15.2 %all-to-all-start.3 = ((bf16[1,2,512,128]{3,1,0,2:T(2,128)(2,1)}), bf16[1,2,512,128]{3,1,0,2:T(2,128)(2,1)S(1)}, u32[]{:S(2)}, u32[]{:S(2)}) async-start(bf16[1,2,512,128]{3,1,0,2:T(2,128)(2,1)} %copy.180), calls=%async_computation.3 | async-start | bytes 524288 | tf_op jit(solution)/shard_map/all_to_all | solution.py:133
  92.3 13.4 %all-to-all-start.1 = ((bf16[2,2,512,128]{3,1,0,2:T(2,128)(2,1)}), bf16[2,2,512,128]{3,1,0,2:T(2,128)(2,1)S(1)}, u32[]{:S(2)}, u32[]{:S(2)}) async-start(bf16[2,2,512,128]{3,1,0,2:T(2,128)(2,1)} %pad_maximum_fusion.2), calls=%async_computation.1 | async-start | bytes 1048576 | tf_op jit(solution)/shard_map/all_to_all | solution.py:132
  120.4 14.6 %all-to-all-start.4 = ((bf16[16,2,8192]{2,1,0:T(2,128)(2,1)}), bf16[16,2,8192]{2,1,0:T(2,128)(2,1)S(1)}, u32[]{:S(2)}, u32[]{:S(2)}) async-start(bf16[16,2,8192]{2,1,0:T(2,128)(2,1)} %reshape.235), calls=%async_computation.4 | async-start | bytes 1048576 | tf_op jit(solution)/shard_map/all_to_all | solution.py:139
  179.8 18.6 %collective-permute-start = (bf16[2,4,16,16,1]{4,3,2,1,0:T(8,128)(2,1)S(1)}, bf16[2,4,16,16,1]{4,3,2,1,0:T(8,128)(2,1)S(1)}, u32[]{:S(2)}, u32[]{:S(2)}) collective-permute-start(bf16[2,4,16,16,1]{4,3,2,1,0:T(8,128)(2,1)S(1)} %get-tuple-element.27), channel_id=1, source_target_pairs={{0,32},{32,64},{64,96},{96,128},{128,160},{160,192},{192,224},{224... | collective-permute-start | bytes 12296 | tf_op jit(solution)/shard_map/ppermute | solution.py:18
  185.3 13.0 %collective-permute-start.1 = (bf16[2,4,16,16,1]{4,3,2,1,0:T(8,128)(2,1)S(1)}, bf16[2,4,16,16,1]{4,3,2,1,0:T(8,128)(2,1)S(1)}, u32[]{:S(2)}, u32[]{:S(2)}) collective-permute-start(bf16[2,4,16,16,1]{4,3,2,1,0:T(8,128)(2,1)S(1)} %get-tuple-element.28), channel_id=1, source_target_pairs={{32,0},{64,32},{96,64},{128,96},{160,128},{192,160},{224,192},{256... | collective-permute-start | bytes 12296 | tf_op jit(solution)/shard_map/ppermute | solution.py:21
  199.2 5.1 %collective-permute-start.2 = (bf16[2,4,16,1,130]{4,3,2,1,0:T(2,128)(2,1)S(1)}, bf16[2,4,16,1,130]{4,3,2,1,0:T(2,128)(2,1)S(1)}, u32[]{:S(2)}, u32[]{:S(2)}) collective-permute-start(bf16[2,4,16,1,130]{4,3,2,1,0:T(2,128)(2,1)S(1)} %get-tuple-element.25), channel_id=1, source_target_pairs={{0,1},{1,2},{2,3},{3,4},{4,5},{5,6},{6,7},{7,8},{8,9},{9,10},{10,1... | collective-permute-start | bytes 99848 | tf_op jit(solution)/shard_map/ppermute | solution.py:18
  202.4 7.2 %collective-permute-start.3 = (bf16[2,4,16,1,130]{4,3,2,1,0:T(2,128)(2,1)S(1)}, bf16[2,4,16,1,130]{4,3,2,1,0:T(2,128)(2,1)S(1)}, u32[]{:S(2)}, u32[]{:S(2)}) collective-permute-start(bf16[2,4,16,1,130]{4,3,2,1,0:T(2,128)(2,1)S(1)} %get-tuple-element.26), channel_id=1, source_target_pairs={{1,0},{2,1},{3,2},{4,3},{5,4},{6,5},{7,6},{8,7},{9,8},{10,9},{11,1... | collective-permute-start | bytes 99848 | tf_op jit(solution)/shard_map/ppermute | solution.py:21
where the time goes:
time: 216 us; the launch traced here: 213 us
  waiting for transfers between devices  84.1 us (39%)
  starting transfers between devices  52.3 us (24%)
  blocking collectives  35.7 us (17%)
  other arithmetic  16.6 us (8%)
  local copies, waits for them, and re-layouts  16 us (7%)
  matrix products  8.21 us (4%)
    all_to_all x1, blocking collectives, local(): lax.all_to_all(spatial, 'gy', split_axis=2, concat_axis=1, tiled=True)  35.7 us
    all_to_all x1, waiting for transfers between devices, local(): lax.all_to_all(volume, 'gy', split_axis=1, concat_axis=2, tiled=True)  29.5 us
    all_to_all x1, waiting for transfers between devices, local(): lax.all_to_all(slice_phase.astype(jnp.bfloat16), 'gy', split_axis=1, conc...  18.8 us
    all_to_all x1, starting transfers between devices, local(): lax.all_to_all(slice_phase.astype(jnp.bfloat16), 'gy', split_axis=1, conc...  18.7 us
    ppermute x2, waiting for transfers between devices, with_halo(): lax.ppermute(lax.slice_in_dim(block, block.shape[dim] - width, None, axis...  11.7 us
    all_to_all x1, waiting for transfers between devices, local(): lax.all_to_all(pencil, 'gx', split_axis=3, concat_axis=2, tiled=True)  9.52 us
    ppermute x2, starting transfers between devices, with_halo(): lax.ppermute(lax.slice_in_dim(block, block.shape[dim] - width, None, axis...  8.78 us
    all_to_all x1, starting transfers between devices, local(): lax.all_to_all(phase_lines.astype(jnp.bfloat16), 'gx', split_axis=2, conc...  7.79 us
  transfers between devices with their start and end apart: 9, of which 8 were waited for; matrix products, arithmetic and copies ran while one was open for 5% of the time, Pallas kernels for 0%

commit v1 on v0

v1 whole, which is shorter than its diff:
```python
import functools

import jax
import jax.numpy as jnp
import ml_dtypes
import numpy as np
from jax import lax
from jax.experimental import pallas as pl
from jax.experimental.pallas import tpu as pltpu
from jax.sharding import PartitionSpec as P


MESH = pl.DeviceIdType.MESH
BF = jnp.bfloat16
F32 = jnp.float32
GX = 16
GY = 32
P0, P1, T0, T2, T3, T5 = 0, 1, 2, 4, 6, 8


def stacked(matrix):
    return np.block([[matrix.real, -matrix.imag], [matrix.imag, matrix.real]])


def constant_tables():
    k4 = np.arange(4)[:, None, None]
    i128 = np.arange(128)
    low = np.exp(-2j * np.pi * (i128[:, None] * i128[None, :] % 128) / 128)
    twist = np.exp(-2j * np.pi * (np.arange(4)[:, None] * i128[None, :] % 512) / 512)
    del k4
    wy = np.stack([stacked(low.T * twist[k][None, :]) for k in range(4)])
    wyi = np.stack([stacked((low.conj() * twist[k].conj()[None, :]).T / 512) for k in range(4)])
    wx = stacked(low).T
    wxi = stacked(low.conj() / 2048).T
    tw = np.exp(-2j * np.pi * (np.arange(16)[:, None] * i128[None, :] % 2048) / 2048)
    bf = ml_dtypes.bfloat16
    return (
        wy.astype(bf),
        wyi.astype(bf),
        np.stack([wx, wxi]).astype(bf),
        np.stack([tw.real, tw.imag]).astype(np.float32),
    )


def dft4(x, q):
    (ar, ai), (br, bi), (cr, ci), (dr, di) = x
    sr, si, tr, ti = ar + cr, ai + ci, ar - cr, ai - ci
    ur, ui, vr, vi = br + dr, bi + di, br - dr, bi - di
    minus = (tr + vi, ti - vr)
    plus = (tr - vi, ti + vr)
    first, third = (minus, plus) if q < 0 else (plus, minus)
    return [(sr + ur, si + ui), first, (sr - ur, si - ui), third]


def dft16(x, q):
    inner = [dft4([x[4 * n + b] for n in range(4)], q) for b in range(4)]
    out = [None] * 16
    for c in range(4):
        column = []
        for b in range(4):
            re, im = inner[b][c]
            if b * c:
                angle = 2 * np.pi * b * c / 16
                wr = float(np.float32(np.cos(angle)).astype(ml_dtypes.bfloat16))
                wi = float(np.float32(q * np.sin(angle)).astype(ml_dtypes.bfloat16))
                if abs(wr) < 1e-6:
                    re, im = (-im, re) if wi > 0 else (im, -re)
                else:
                    re, im = re * wr - im * wi, re * wi + im * wr
            column.append((re, im))
        for d, value in enumerate(dft4(column, q)):
            out[c + 4 * d] = value
    return out


def turn(i, count):
    return lax.rem(i, 2) * ((i + 1) // 2) + (1 - lax.rem(i, 2)) * (count - i // 2)


def kernel(
    vol, pupil, wy_h, wyi_h, wx_h, tw_h, out,
    wy, wyi, wx, tw, ph, ph0, ph1, ph2, cosine, sine,
    buf0, gy_s, send1, buf1, gx_s, cx_s, hx_s, fx_s, send2, buf2, hy_s, stats, send3, buf3,
    ssem, rsem, csem,
):
    a = lax.axis_index("gx")
    g = lax.axis_index("gy")
    z, h = g // 2, lax.rem(g, 2)
    j = 2 * a + h
    lane = lax.broadcasted_iota(jnp.int32, (16, 128), 1)
    low_lane = lane < 64

    loads = [
        pltpu.make_async_copy(s, d, csem.at[n])
        for n, (s, d) in enumerate(
            [(pupil, ph), (wy_h, wy), (wx_h, wx), (tw_h, tw), (wyi_h, wyi)]
        )
    ]
    for copy in loads:
        copy.start()

    barrier = pltpu.get_barrier_semaphore()

    def greet_column(t, _):
        pl.semaphore_signal(
            barrier, inc=1, device_id=(a, lax.rem(g + t, GY)), device_id_type=MESH
        )
        return 0

    def greet_plane(t, _):
        peer = lax.rem(a + t, GX)
        pl.semaphore_signal(barrier, inc=1, device_id=(peer, 2 * z), device_id_type=MESH)
        pl.semaphore_signal(barrier, inc=1, device_id=(peer, 2 * z + 1), device_id_type=MESH)
        return 0

    lax.fori_loop(1, GY, greet_column, 0)
    lax.fori_loop(1, GX, greet_plane, 0)
    loads[0].wait()
    ph0[...] = ph[...].astype(BF)
    pl.semaphore_wait(barrier, 61)

    def remote(src, dst, which, device):
        pltpu.make_async_remote_copy(
            src_ref=src, dst_ref=dst, send_sem=ssem.at[which], recv_sem=rsem.at[which],
            device_id=device, device_id_type=MESH,
        ).start()

    def wait(sem, ref):
        pltpu.make_async_copy(ref, ref, sem).wait()

    def send_p0(t, _):
        zt = lax.rem(z + turn(t, 16), 16)
        remote(ph0.at[zt], ph1.at[z], P0, (a, 2 * zt + h))
        return 0

    lax.fori_loop(1, 16, send_p0, 0)
    pltpu.make_async_copy(ph0.at[z], ph1.at[z], rsem.at[P0]).start()

    for i in range(2):
        def send_t0(t, _, i=i):
            gt = lax.rem(g + turn(t, GY), GY)
            zt, ht = gt // 2, lax.rem(gt, 2)
            remote(vol.at[:, 2 * ht + i, zt], buf0.at[i, :, g], T0 + i, (a, gt))
            return 0

        lax.fori_loop(1, GY, send_t0, 0)
        pltpu.make_async_copy(
            vol.at[:, 2 * h + i, z], buf0.at[i, :, g], rsem.at[T0 + i]
        ).start()

    wait(rsem.at[P0], ph1)

    def send_p1(t, _):
        at = lax.rem(a + turn(t, 16), 16)
        remote(ph1.at[at], ph2.at[a], P1, (at, g))
        return 0

    lax.fori_loop(1, 16, send_p1, 0)
    pltpu.make_async_copy(ph1.at[a], ph2.at[a], rsem.at[P1]).start()
    for copy in loads[1:]:
        copy.wait()
    wait(rsem.at[P1], ph2)

    def angles(k, _):
        phase = ph2[k].astype(F32)
        cosine[k] = jnp.cos(phase)
        sine[k] = jnp.sin(phase)
        return 0

    lax.fori_loop(0, 16, angles, 0)

    def x_stage(i):
        for s in range(2):
            x = [
                (buf1[i, 2 * n + s, 0].astype(F32), buf1[i, 2 * n + s, 1].astype(F32))
                for n in range(16)
            ]
            for k, (re, im) in enumerate(dft16(x, -1)):
                c, w = tw[0, k : k + 1, :], tw[1, k : k + 1, :]
                row = pl.ds(32 * k + 16 * s, 16)
                gx_s[row, 0:128] = (re * c - im * w).astype(BF)
                gx_s[row, 128:256] = (re * w + im * c).astype(BF)
        for b in range(4):
            rows = pl.ds(128 * b, 128)
            f = jnp.dot(gx_s[rows, :], wx[0], preferred_element_type=F32)
            for n in range(8):
                k = 4 * b + n // 2
                re, im = f[16 * n : 16 * n + 16, 0:128], f[16 * n : 16 * n + 16, 128:256]
                row = pl.ds(128 * b + 16 * n, 16)
                cx_s[row, 0:128] = (re * cosine[k] - im * sine[k]).astype(BF)
                cx_s[row, 128:256] = (re * sine[k] + im * cosine[k]).astype(BF)
            hx_s[rows, :] = jnp.dot(cx_s[rows, :], wx[1], preferred_element_type=F32)
        for s in range(2):
            x = []
            for k in range(16):
                c, w = tw[0, k : k + 1, :], tw[1, k : k + 1, :]
                row = pl.ds(32 * k + 16 * s, 16)
                re, im = hx_s[row, 0:128], hx_s[row, 128:256]
                x.append((re * c + im * w, im * c - re * w))
            for n, (re, im) in enumerate(dft16(x, 1)):
                fx_s[s, 0, n] = re
                fx_s[s, 1, n] = im

        def tiles(n, c):
            one, two = fx_s[0, c, n], fx_s[1, c, n]
            turned_one, turned_two = pltpu.roll(one, 64, 1), pltpu.roll(two, 64, 1)
            return one, two, turned_one, turned_two

        at_edge = (lane == 0) | (lane == 63) | (lane == 64) | (lane == 127)
        near = (lane == 0) | (lane == 64)

        def pack(n, _):
            before, after = lax.rem(n + 15, 16), lax.rem(n + 1, 16)
            rims = []
            for c in range(2):
                one, two, turned_one, turned_two = tiles(n, c)
                send2[i, 2 * n, c] = jnp.where(low_lane, one, turned_two).astype(BF)
                send2[i, 2 * n + 1, c] = jnp.where(low_lane, turned_one, two).astype(BF)
                upper = jnp.where(low_lane, turned_two, one)
                lower = jnp.where(low_lane, two, turned_one)
                one, _, _, turned_two = tiles(before, c)
                upper_before = jnp.where(low_lane, turned_two, one)
                _, two, turned_one, _ = tiles(after, c)
                lower_after = jnp.where(low_lane, two, turned_one)
                rims.append(
                    (jnp.where(near, upper, upper_before), jnp.where(near, lower_after, lower))
                )
            for half in range(2):
                send2[i, 2 * n + half, 2] = jnp.where(
                    at_edge, rims[0][half], pltpu.roll(rims[1][half], 2, 1)
                ).astype(BF)
            return 0

        lax.fori_loop(0, 16, pack, 0)

    def plane_device(t):
        jt = lax.rem(j + turn(t, 32), 32)
        return jt, (jt // 2, 2 * z + lax.rem(jt, 2))

    for i in range(2):
        wait(rsem.at[T0 + i], buf0.at[i])

        def columns(n, _, i=i):
            x = [
                (buf0[i, 0, 8 * m + n].astype(F32), buf0[i, 1, 8 * m + n].astype(F32))
                for m in range(4)
            ]
            row = pl.multiple_of(16 * n, 16)
            for k, (re, im) in enumerate(dft4(x, -1)):
                gy_s[k, pl.ds(row, 16), :] = re.astype(BF)
                gy_s[k, pl.ds(128 + row, 16), :] = im.astype(BF)
            return 0

        lax.fori_loop(0, 8, columns, 0)
        for k in range(4):
            f = jnp.dot(wy[k], gy_s[k], preferred_element_type=F32).astype(BF)
            send1[i, 8 * k : 8 * k + 8, 0] = f[0:128].reshape(8, 16, 128)
            send1[i, 8 * k : 8 * k + 8, 1] = f[128:256].reshape(8, 16, 128)

        def send_t2(t, _, i=i):
            jt, device = plane_device(t)
            remote(send1.at[i, jt], buf1.at[i, j], T2 + i, device)
            return 0

        lax.fori_loop(1, 32, send_t2, 0)
        pltpu.make_async_copy(send1.at[i, j], buf1.at[i, j], rsem.at[T2 + i]).start()
        wait(rsem.at[T2 + i], buf1.at[i])

        x_stage(i)

        def send_t3(t, _, i=i):
            jt, device = plane_device(t)
            remote(
                send2.at[i, jt], buf2.at[i, j // 8, :, lax.rem(j, 8)], T3 + i, device
            )
            return 0

        lax.fori_loop(1, 32, send_t3, 0)
        pltpu.make_async_copy(
            send2.at[i, j], buf2.at[i, j // 8, :, lax.rem(j, 8)], rsem.at[T3 + i]
        ).start()
        wait(rsem.at[T3 + i], buf2.at[i])

        for k in range(4):
            main = jnp.concatenate(
                [buf2[i, k, 0].reshape(128, 128), buf2[i, k, 1].reshape(128, 128)], axis=0
            )
            rim = buf2[i, k, 2].reshape(128, 128)
            rim_im = pltpu.roll(rim.astype(F32), 126, 1).astype(BF)
            both = jnp.concatenate([main, jnp.concatenate([rim, rim_im], axis=0)], axis=1)
            hy_s[i, k] = jnp.dot(wyi[k], both, preferred_element_type=F32)

    keep_left = jnp.where((a == 0) & (h == 0), 0.0, 1.0)
    keep_right = jnp.where((a == 15) & (h == 1), 0.0, 1.0)
    rim_mask = jnp.where(lane == 127, keep_left, jnp.where(lane == 64, keep_right, 1.0))
    is_rim = (lane == 127) | (lane == 64)

    stats[:, 0:8, :] = jnp.zeros((3, 8, 128), F32)
    stats[:, 520:528, :] = jnp.zeros((3, 8, 128), F32)

    def pair(ar, ai, br, bi):
        tr, ti = pltpu.roll(ar, 64, 1), pltpu.roll(ai, 64, 1)
        pr, pi = ar * br + ai * bi, ai * br - ar * bi
        u, v = ar * ar + ai * ai, br * br + bi * bi
        return (
            pr + pltpu.roll(pr, 64, 1) + (br * tr + bi * ti),
            pi + pltpu.roll(pi, 64, 1) + (bi * tr - br * ti),
            (0.5 * u + v) + pltpu.roll(u + 0.5 * v, 64, 1),
        )

    def statistics(n, _):
        row = pl.multiple_of(16 * n, 16)
        fields = []
        for part in range(2):
            cols = pl.ds(128 * part, 128)
            pairs = []
            for i in range(2):
                x = [
                    (hy_s[i, k, pl.ds(row, 16), cols], hy_s[i, k, pl.ds(128 + row, 16), cols])
                    for k in range(4)
                ]
                pairs.append(dft4(x, 1))
            fields.append([pair(*pairs[0][m], *pairs[1][m]) for m in range(4)])
        for m in range(4):
            for s in range(3):
                value = jnp.where(is_rim, fields[1][m][s] * rim_mask, fields[0][m][s])
                value = value + pltpu.roll(value, 1, 1) + pltpu.roll(value, 127, 1)
                stats[s, pl.ds(pl.multiple_of(8 + 128 * m + row, 8), 16), :] = value
        return 0

    lax.fori_loop(0, 8, statistics, 0)

    wide_low = lax.broadcasted_iota(jnp.int32, (128, 128), 1) < 64
    for m in range(4):
        sums = []
        for s in range(3):
            base = 8 + 128 * m
            sums.append(
                stats[s, base - 1 : base + 127, :]
                + stats[s, base : base + 128, :]
                + stats[s, base + 1 : base + 129, :]
            )
        cross = jnp.where(wide_low, sums[0], pltpu.roll(sums[1], 64, 1)).astype(BF)
        energy = jnp.where(wide_low, sums[2], pltpu.roll(sums[2], 64, 1)).astype(BF)
        send3[8 * m : 8 * m + 8, 0] = cross.reshape(8, 16, 128)
        send3[8 * m : 8 * m + 8, 1] = energy.reshape(8, 16, 128)

    def send_t5(t, _):
        gt = lax.rem(g + turn(t, GY), GY)
        remote(send3.at[gt], buf3.at[g], T5, (a, gt))
        return 0

    lax.fori_loop(1, GY, send_t5, 0)
    pltpu.make_async_copy(send3.at[g], buf3.at[g], rsem.at[T5]).start()
    wait(rsem.at[T5], buf3)

    def depth(d):
        c0, c1 = buf3[2 * d, 0].astype(F32), buf3[2 * d + 1, 0].astype(F32)
        e = jnp.where(low_lane, buf3[2 * d, 1].astype(F32), buf3[2 * d + 1, 1].astype(F32))
        return c0, c1, e

    window = [None, depth(0), depth(1)]
    for d in range(16):
        present = [w for w in window if w is not None]
        c0, c1, e = [functools.reduce(jnp.add, terms) for terms in zip(*present)]
        s0, s1 = c0 * c0, c1 * c1
        s0, s1 = s0 + pltpu.roll(s0, 64, 1), s1 + pltpu.roll(s1, 64, 1)
        magnitude = jnp.sqrt(jnp.where(low_lane, s0, s1))
        out[d] = 1.0 - magnitude / (e + 1e-6)
        window = window[1:] + [depth(d + 2) if d + 2 < 16 else None]

    wait(ssem.at[P0], ph1.at[0:15])
    wait(ssem.at[P1], ph2.at[0:15])
    for i in range(2):
        wait(ssem.at[T0 + i], buf1.at[i, 0:31])
        wait(ssem.at[T2 + i], buf1.at[i, 0:31])
        wait(ssem.at[T3 + i], send2.at[i, 0:31])
    wait(ssem.at[T5], buf3.at[0:31])


def local(volume, pupil_phase):
    wy, wyi, wx, tw = constant_tables()
    vm = pltpu.VMEM
    return pl.pallas_call(
        kernel,
        out_shape=jax.ShapeDtypeStruct((16, 16, 128), F32),
        in_specs=[pl.BlockSpec(memory_space=pl.ANY)] * 6,
        out_specs=pl.BlockSpec(memory_space=pltpu.VMEM),
        scratch_shapes=[
            vm((4, 256, 256), BF),
            vm((4, 256, 256), BF),
            vm((2, 256, 256), BF),
            vm((2, 16, 128), F32),
            vm((16, 16, 128), F32),
            vm((16, 16, 128), BF),
            vm((16, 16, 128), BF),
            vm((16, 16, 128), BF),
            vm((16, 16, 128), F32),
            vm((16, 16, 128), F32),
            vm((2, 2, 32, 16, 128), BF),
            vm((4, 256, 128), BF),
            vm((2, 32, 2, 16, 128), BF),
            vm((2, 32, 2, 16, 128), BF),
            vm((512, 256), BF),
            vm((512, 256), BF),
            vm((512, 256), F32),
            vm((2, 2, 16, 16, 128), F32),
            vm((2, 32, 3, 16, 128), BF),
            vm((2, 4, 3, 8, 16, 128), BF),
            vm((2, 4, 256, 256), F32),
            vm((3, 528, 128), F32),
            vm((32, 2, 16, 128), BF),
            vm((32, 2, 16, 128), BF),
            pltpu.SemaphoreType.DMA((9,)),
            pltpu.SemaphoreType.DMA((9,)),
            pltpu.SemaphoreType.DMA((5,)),
        ],
        compiler_params=pltpu.CompilerParams(
            collective_id=0, has_side_effects=True, vmem_limit_bytes=40 * 1024 * 1024
        ),
        name="decorrelation",
    )(
        volume.reshape(2, 4, 16, 16, 128),
        pupil_phase,
        jnp.asarray(wy),
        jnp.asarray(wyi),
        jnp.asarray(wx),
        jnp.asarray(tw),
    )


def solution(mesh):
    return jax.shard_map(
        local,
        mesh=mesh,
        in_specs=(P(None, None, "gy", "gx"), P(None, "gy", "gx")),
        out_specs=P(None, "gy", "gx"),
        check_vma=False,
    )
```

time: 216 us -> 103 us (0.48)
  Pallas kernels: 0 us -> 95.1 us
  waiting for transfers between devices: 84.1 us -> 0 us
  starting transfers between devices: 52.3 us -> 0 us
  blocking collectives: 35.7 us -> 0 us
  other arithmetic: 16.6 us -> 0 us
  local copies, waits for them, and re-layouts: 16 us -> 6.35 us
  matrix products: 8.21 us -> 0 us
    pallas_call x0 -> x1, Pallas kernels: none -> 95.1 us  [local(): pl.pallas_call(kernel, out_shape=jax.ShapeDtypeStruct((16, 16, 128), F32)...]
    all_to_all x5 -> x0, waiting for transfers between devices: 67.1 us -> none  [the longest x1 29.5 us: local(): lax.all_to_all(volume, 'gy', split_axis=1, concat_axis=2, tiled=True)]
    all_to_all x5 -> x0, starting transfers between devices: 40.3 us -> none  [the longest x1 18.7 us: local(): lax.all_to_all(slice_phase.astype(jnp.bfloat16), 'gy', split_axis=1, conc...]
    all_to_all x1 -> x0, blocking collectives: 35.7 us -> none  [local(): lax.all_to_all(spatial, 'gy', split_axis=2, concat_axis=1, tiled=True)]
    ppermute x4 -> x0, waiting for transfers between devices: 17 us -> none  [the longest x2 11.7 us: with_halo(): lax.ppermute(lax.slice_in_dim(block, block.shape[dim] - width, None, axis...]
    ppermute x4 -> x0, starting transfers between devices: 12 us -> none  [the longest x2 8.78 us: with_halo(): lax.ppermute(lax.slice_in_dim(block, block.shape[dim] - width, None, axis...]
    dot_general x16 -> x0, matrix products: 8.21 us -> none  [the longest x8 4.11 us: contract(): jnp.einsum(pattern, fields, sine_table, preferred_element_type=jnp.float32)]
    another operation x14 -> x0, other arithmetic: 7.93 us -> none
  transfers between devices with their start and end apart: 9 -> 0, of which waited for: 8 -> 0; matrix products, arithmetic and copies ran while one was open for 5% -> 0% of each run, Pallas kernels for 0% -> 0%
where the time goes in v1:
time: 103 us; the launch traced here: 101 us
  Pallas kernels  95.1 us (92%)
  local copies, waits for them, and re-layouts  6.35 us (6%)
    pallas_call x1, Pallas kernels, local(): pl.pallas_call(kernel, out_shape=jax.ShapeDtypeStruct((16, 16, 128), F32)...  95.1 us
    unnamed x13, local copies, waits for them, and re-layouts  6.35 us

profile of v1, /device:TPU:1, one launch (start us, length us, event | category | flops | bytes accessed | tf_op | source)
XLA Modules:
  0.0 101.4 jit_solution(6639104595023439774)
XLA Ops:
  0.0 0.0 copy-start
  0.0 1.0 %copy-done = bf16[2,64,16,128]{3,2,1,0:T(8,128)(2,1)S(1)} copy-done((bf16[2,64,16,128]{3,2,1,0:T(8,128)(2,1)S(1)}, bf16[2,64,16,128]{3,2,1,0:T(8,128)(2,1)}, u32[]{:S(2)}) %copy-start) | copy-done | bytes 524312
  1.0 0.0 copy-start.1
  1.0 1.0 %copy-done.1 = bf16[4,256,256]{2,1,0:T(8,128)(2,1)S(1)} copy-done((bf16[4,256,256]{2,1,0:T(8,128)(2,1)S(1)}, bf16[4,256,256]{2,1,0:T(8,128)(2,1)}, u32[]{:S(2)}) %copy-start.1) | copy-done | bytes 524312
  2.1 0.0 copy-start.2
  2.1 1.0 %copy-done.2 = bf16[4,256,256]{2,1,0:T(8,128)(2,1)S(1)} copy-done((bf16[4,256,256]{2,1,0:T(8,128)(2,1)S(1)}, bf16[4,256,256]{2,1,0:T(8,128)(2,1)}, u32[]{:S(2)}) %copy-start.2) | copy-done | bytes 524312
  3.1 0.0 copy-start.3
  3.1 0.9 copy-done.3
  4.1 0.0 copy-start.4
  4.1 0.9 copy-done.4
  5.0 0.0 copy-start.5
  5.0 0.7 copy-done.5
  5.7 95.1 %decorrelation.1 = f32[16,16,128]{2,1,0:T(8,128)S(1)} custom-call(bf16[2,4,16,16,128]{4,3,2,1,0:T(8,128)(2,1)S(1)} %bitcast.1, f32[16,16,128]{2,1,0:T(8,128)S(1)} %copy-done.4, bf16[4,256,256]{2,1,0:T(8,128)(2,1)S(1)} %copy-done.2, bf16[4,256,256]{2,1,0:T(8,128)(2,1)S(1)} %copy-done.1, bf16[2,256,256]{2,1,0:T(8,128)(2,1)S(1)} %copy-done.3, ...), custom_call_target="tpu_custom_call" | custom-call | tf_op jit(solution)/shard_map/decorrelation/pallas_call | solution.py:384
  100.8 0.7 copy.8
Async XLA Ops:
  0.0 1.0 %copy-start = (bf16[2,64,16,128]{3,2,1,0:T(8,128)(2,1)S(1)}, bf16[2,64,16,128]{3,2,1,0:T(8,128)(2,1)}, u32[]{:S(2)}) copy-start(bf16[2,64,16,128]{3,2,1,0:T(8,128)(2,1)} %param.6) | copy-start | bytes 1572868
  1.0 1.0 %copy-start.1 = (bf16[4,256,256]{2,1,0:T(8,128)(2,1)S(1)}, bf16[4,256,256]{2,1,0:T(8,128)(2,1)}, u32[]{:S(2)}) copy-start(bf16[4,256,256]{2,1,0:T(8,128)(2,1)} %constant.9.clone.wyi_h) | copy-start | bytes 1572868
  2.1 1.0 %copy-start.2 = (bf16[4,256,256]{2,1,0:T(8,128)(2,1)S(1)}, bf16[4,256,256]{2,1,0:T(8,128)(2,1)}, u32[]{:S(2)}) copy-start(bf16[4,256,256]{2,1,0:T(8,128)(2,1)} %constant.8.clone.wy_h) | copy-start | bytes 1572868
  3.1 0.9 copy-start.3
  4.1 0.9 copy-start.4
  5.0 0.7 copy-start.5

commit v2 on v1

v2 whole, which is shorter than its diff:
```python
import functools

import jax
import jax.numpy as jnp
import ml_dtypes
import numpy as np
from jax import lax
from jax.experimental import pallas as pl
from jax.experimental.pallas import tpu as pltpu
from jax.sharding import PartitionSpec as P


MESH = pl.DeviceIdType.MESH
BF = jnp.bfloat16
F32 = jnp.float32
GX = 16
GY = 32
P0, P1, T0, T2, T3, T5 = 0, 1, 2, 4, 6, 8
EARLY = 16


def stacked(matrix):
    return np.block([[matrix.real, -matrix.imag], [matrix.imag, matrix.real]])


def constant_tables():
    i128 = np.arange(128)
    low = np.exp(-2j * np.pi * (i128[:, None] * i128[None, :] % 128) / 128)
    twist = np.exp(-2j * np.pi * (np.arange(4)[:, None] * i128[None, :] % 512) / 512)
    wy = np.stack([stacked(low.T * twist[k][None, :]) for k in range(4)])
    wyi = np.stack([stacked((low.conj() * twist[k].conj()[None, :]).T / 512) for k in range(4)])
    back = low.conj() / 2048
    wx = np.stack([stacked(m.T).T for m in (low, back, np.roll(back, 64, axis=1))])
    tw = np.exp(-2j * np.pi * (np.arange(16)[:, None] * i128[None, :] % 2048) / 2048)
    turned = np.roll(tw, 64, axis=1)
    bf = ml_dtypes.bfloat16
    return (
        wy.astype(bf),
        wyi.astype(bf),
        wx.astype(bf),
        np.stack([tw.real, tw.imag, turned.real, turned.imag]).astype(np.float32),
    )


def dft4(x, q):
    (ar, ai), (br, bi), (cr, ci), (dr, di) = x
    sr, si, tr, ti = ar + cr, ai + ci, ar - cr, ai - ci
    ur, ui, vr, vi = br + dr, bi + di, br - dr, bi - di
    minus = (tr + vi, ti - vr)
    plus = (tr - vi, ti + vr)
    first, third = (minus, plus) if q < 0 else (plus, minus)
    return [(sr + ur, si + ui), first, (sr - ur, si - ui), third]


def dft16(x, q):
    inner = [dft4([x[4 * n + b] for n in range(4)], q) for b in range(4)]
    out = [None] * 16
    for c in range(4):
        column = []
        for b in range(4):
            re, im = inner[b][c]
            if b * c:
                angle = 2 * np.pi * b * c / 16
                wr = float(np.float32(np.cos(angle)).astype(ml_dtypes.bfloat16))
                wi = float(np.float32(q * np.sin(angle)).astype(ml_dtypes.bfloat16))
                if abs(wr) < 1e-6:
                    re, im = (-im, re) if wi > 0 else (im, -re)
                else:
                    re, im = re * wr - im * wi, re * wi + im * wr
            column.append((re, im))
        for d, value in enumerate(dft4(column, q)):
            out[c + 4 * d] = value
    return out


def turn(i, count):
    return lax.rem(i, 2) * ((i + 1) // 2) + (1 - lax.rem(i, 2)) * (count - i // 2)


def kernel(
    vol, pupil, wy_h, wyi_h, wx_h, tw_h, out,
    wy, wyi, wx, tw, ph, ph0, ph1, ph2, cosine, sine,
    buf0, gy_s, send1, buf1, gx_s, cx_s, hx_s, fx_s, send2, buf2, hy_s, stats, send3, buf3,
    ssem, rsem, csem,
):
    a = lax.axis_index("gx")
    g = lax.axis_index("gy")
    z, h = g // 2, lax.rem(g, 2)
    j = 2 * a + h
    lane = lax.broadcasted_iota(jnp.int32, (16, 128), 1)
    low_lane = lane < 64

    loads = [
        pltpu.make_async_copy(s, d, csem.at[n])
        for n, (s, d) in enumerate(
            [(pupil, ph), (wy_h, wy), (wx_h, wx), (tw_h, tw), (wyi_h, wyi)]
        )
    ]
    for copy in loads:
        copy.start()

    barrier = pltpu.get_barrier_semaphore()

    def greet_column(t, _):
        pl.semaphore_signal(
            barrier, inc=1, device_id=(a, lax.rem(g + t, GY)), device_id_type=MESH
        )
        return 0

    def greet_plane(t, _):
        peer = lax.rem(a + t, GX)
        pl.semaphore_signal(barrier, inc=1, device_id=(peer, 2 * z), device_id_type=MESH)
        pl.semaphore_signal(barrier, inc=1, device_id=(peer, 2 * z + 1), device_id_type=MESH)
        return 0

    lax.fori_loop(1, GY, greet_column, 0)
    lax.fori_loop(1, GX, greet_plane, 0)
    loads[0].wait()
    ph0[...] = ph[...].astype(BF)
    pl.semaphore_wait(barrier, 61)

    def remote(src, dst, which, device):
        pltpu.make_async_remote_copy(
            src_ref=src, dst_ref=dst, send_sem=ssem.at[which], recv_sem=rsem.at[which],
            device_id=device, device_id_type=MESH,
        ).start()

    def wait(sem, ref):
        pltpu.make_async_copy(ref, ref, sem).wait()

    def send_p0(t, _):
        zt = lax.rem(z + turn(t, 16), 16)
        remote(ph0.at[zt], ph1.at[z], P0, (a, 2 * zt + h))
        return 0

    lax.fori_loop(1, 16, send_p0, 0)
    pltpu.make_async_copy(ph0.at[z], ph1.at[z], rsem.at[P0]).start()

    def send_t0(i, first, last):
        def step(t, _):
            gt = lax.rem(g + turn(t, GY), GY)
            zt, ht = gt // 2, lax.rem(gt, 2)
            remote(vol.at[:, 2 * ht + i, zt], buf0.at[i, :, g], T0 + i, (a, gt))
            return 0

        lax.fori_loop(first, last, step, 0)

    def keep_t0(i):
        pltpu.make_async_copy(
            vol.at[:, 2 * h + i, z], buf0.at[i, :, g], rsem.at[T0 + i]
        ).start()

    send_t0(0, 1, GY)
    keep_t0(0)
    keep_t0(1)

    wait(rsem.at[P0], ph1)

    def send_p1(t, _):
        at = lax.rem(a + turn(t, 16), 16)
        remote(ph1.at[at], ph2.at[a], P1, (at, g))
        return 0

    lax.fori_loop(1, 16, send_p1, 0)
    pltpu.make_async_copy(ph1.at[a], ph2.at[a], rsem.at[P1]).start()
    send_t0(1, 1, 1 + EARLY)
    for copy in loads[1:]:
        copy.wait()
    wait(rsem.at[P1], ph2)

    def angles(k, _):
        phase = ph2[k].astype(F32)
        cosine[k] = jnp.cos(phase)
        sine[k] = jnp.sin(phase)
        return 0

    lax.fori_loop(0, 16, angles, 0)

    def y_forward(i):
        def columns(n, _):
            x = [
                (buf0[i, 0, 8 * m + n].astype(F32), buf0[i, 1, 8 * m + n].astype(F32))
                for m in range(4)
            ]
            row = pl.multiple_of(16 * n, 16)
            for k, (re, im) in enumerate(dft4(x, -1)):
                gy_s[k, pl.ds(row, 16), :] = re.astype(BF)
                gy_s[k, pl.ds(128 + row, 16), :] = im.astype(BF)
            return 0

        lax.fori_loop(0, 8, columns, 0)
        for k in range(4):
            f = jnp.dot(wy[k], gy_s[k], preferred_element_type=F32).astype(BF)
            send1[i, 8 * k : 8 * k + 8, 0] = f[0:128].reshape(8, 16, 128)
            send1[i, 8 * k : 8 * k + 8, 1] = f[128:256].reshape(8, 16, 128)

    def send_t2(i):
        def step(t, _):
            jt = lax.rem(j + turn(t, 32), 32)
            remote(send1.at[i, jt], buf1.at[i, j], T2 + i, (jt // 2, 2 * z + lax.rem(jt, 2)))
            return 0

        lax.fori_loop(1, 32, step, 0)
        pltpu.make_async_copy(send1.at[i, j], buf1.at[i, j], rsem.at[T2 + i]).start()

    def x_transforms(i):
        for s in range(2):
            for p in range(2):
                half = slice(8 * p, 8 * p + 8)
                x = [
                    tuple(buf1[i, 2 * n + s, c].astype(F32)[half] for c in range(2))
                    for n in range(16)
                ]
                for k, (re, im) in enumerate(dft16(x, -1)):
                    row = pl.ds(256 * s + 16 * k + 8 * p, 8)
                    c, w = tw[0, k : k + 1, :], tw[1, k : k + 1, :]
                    gx_s[row, 0:128] = re * c - im * w
                    gx_s[row, 128:256] = re * w + im * c
        for s in range(2):
            for b in range(2):
                rows = pl.ds(256 * s + 128 * b, 128)
                f = jnp.dot(gx_s[rows, :].astype(BF), wx[0], preferred_element_type=F32)
                for n in range(8):
                    k = 8 * b + n
                    re, im = f[16 * n : 16 * n + 16, 0:128], f[16 * n : 16 * n + 16, 128:256]
                    row = pl.ds(256 * s + 16 * k, 16)
                    cx_s[row, 0:128] = (re * cosine[k] - im * sine[k]).astype(BF)
                    cx_s[row, 128:256] = (re * sine[k] + im * cosine[k]).astype(BF)
                hx_s[rows, :] = jnp.dot(cx_s[rows, :], wx[1 + s], preferred_element_type=F32)
        for s in range(2):
            for p in range(2):
                x = []
                for k in range(16):
                    row = pl.ds(256 * s + 16 * k + 8 * p, 8)
                    c, w = tw[2 * s, k : k + 1, :], tw[2 * s + 1, k : k + 1, :]
                    re, im = hx_s[row, 0:128], hx_s[row, 128:256]
                    x.append((re * c + im * w, im * c - re * w))
                for n, (re, im) in enumerate(dft16(x, 1)):
                    fx_s[s, 0, n, 8 * p : 8 * p + 8] = re
                    fx_s[s, 1, n, 8 * p : 8 * p + 8] = im

    near = (lane == 0) | (lane == 64)
    at_edge = near | (lane == 63) | (lane == 127)

    def send_t3(i):
        place = buf2.at[i, j // 8, :, lax.rem(j, 8)]

        def straight(n, c):
            return jnp.where(low_lane, fx_s[0, c, n], fx_s[1, c, n])

        def crossed(n, c):
            return jnp.where(low_lane, fx_s[1, c, n], fx_s[0, c, n])

        def pack(n):
            before, after = lax.rem(n + 15, 16), lax.rem(n + 1, 16)
            rims = []
            for c in range(2):
                one, two = straight(n, c), crossed(n, c)
                send2[i, 2 * n, c] = one.astype(BF)
                send2[i, 2 * n + 1, c] = two.astype(BF)
                rims.append(
                    (
                        jnp.where(near, two, crossed(before, c)),
                        jnp.where(near, straight(after, c), one),
                    )
                )
            for half in range(2):
                send2[i, 2 * n + half, 2] = jnp.where(
                    at_edge, rims[0][half], pltpu.roll(rims[1][half], 2, 1)
                ).astype(BF)

        def step(t, _):
            n = lax.rem(a + turn(t, 16), 16)
            pack(n)
            for half in range(2):
                remote(send2.at[i, 2 * n + half], place, T3 + i, (n, 2 * z + half))
            return 0

        lax.fori_loop(1, 16, step, 0)
        pack(a)
        remote(send2.at[i, 2 * a + 1 - h], place, T3 + i, (a, 2 * z + 1 - h))
        pltpu.make_async_copy(send2.at[i, j], place, rsem.at[T3 + i]).start()

    def y_inverse(i):
        for k in range(4):
            main = jnp.concatenate(
                [buf2[i, k, 0].reshape(128, 128), buf2[i, k, 1].reshape(128, 128)], axis=0
            )
            rim = buf2[i, k, 2].reshape(128, 128)
            rim_im = pltpu.roll(rim.astype(F32), 126, 1).astype(BF)
            both = jnp.concatenate([main, jnp.concatenate([rim, rim_im], axis=0)], axis=1)
            hy_s[i, k] = jnp.dot(wyi[k], both, preferred_element_type=F32)

    wait(rsem.at[T0], buf0.at[0])
    y_forward(0)
    send_t2(0)
    send_t0(1, 1 + EARLY, GY)
    wait(rsem.at[T2], buf1.at[0])
    x_transforms(0)
    send_t3(0)
    wait(rsem.at[T0 + 1], buf0.at[1])
    y_forward(1)
    send_t2(1)
    wait(rsem.at[T3], buf2.at[0])
    y_inverse(0)
    wait(rsem.at[T2 + 1], buf1.at[1])
    x_transforms(1)
    send_t3(1)
    wait(rsem.at[T3 + 1], buf2.at[1])
    y_inverse(1)

    left, right = jnp.where(h == 0, 127, 63), jnp.where(h == 0, 64, 0)
    keep_left = jnp.where((a == 0) & (h == 0), 0.0, 1.0)
    keep_right = jnp.where((a == 15) & (h == 1), 0.0, 1.0)
    rim_mask = jnp.where(lane == left, keep_left, keep_right)
    is_rim = (lane == left) | (lane == right)
    own = (lane < 64) == (h == 0)

    stats[:, 0:8, :] = jnp.zeros((3, 8, 128), F32)
    stats[:, 520:528, :] = jnp.zeros((3, 8, 128), F32)

    def pair(ar, ai, br, bi):
        tr, ti = pltpu.roll(ar, 64, 1), pltpu.roll(ai, 64, 1)
        pr, pi = ar * br + ai * bi, ai * br - ar * bi
        u, v = ar * ar + ai * ai, br * br + bi * bi
        real = pr + pltpu.roll(pr, 64, 1) + (br * tr + bi * ti)
        energy = (0.5 * u + v) + pltpu.roll(u + 0.5 * v, 64, 1)
        return energy - real, pi + pltpu.roll(pi, 64, 1) + (bi * tr - br * ti), energy

    def statistics(n):
        row = pl.multiple_of(16 * n, 16)
        fields = []
        for part in range(2):
            cols = pl.ds(128 * part, 128)
            pairs = []
            for i in range(2):
                x = [
                    (hy_s[i, k, pl.ds(row, 16), cols], hy_s[i, k, pl.ds(128 + row, 16), cols])
                    for k in range(4)
                ]
                pairs.append(dft4(x, 1))
            fields.append([pair(*pairs[0][m], *pairs[1][m]) for m in range(4)])
        for m in range(4):
            for s in range(3):
                value = jnp.where(is_rim, fields[1][m][s] * rim_mask, fields[0][m][s])
                value = value + pltpu.roll(value, 1, 1) + pltpu.roll(value, 127, 1)
                stats[s, pl.ds(pl.multiple_of(8 + 128 * m + row, 8), 16), :] = value

    def send_t5(n):
        for m in range(4):
            sums = []
            for s in range(3):
                rows = stats[s, pl.ds(pl.multiple_of(128 * m + 16 * n, 8), 32), :]
                sums.append(rows[7:23] + rows[8:24] + rows[9:25])
            gt = 8 * m + n
            send3[gt, 0] = jnp.where(own, sums[0], pltpu.roll(sums[1], 64, 1)).astype(BF)
            send3[gt, 1] = sums[2].astype(BF)

            @pl.when(gt != g)
            def _():
                remote(send3.at[gt], buf3.at[g], T5, (a, gt))

            @pl.when(gt == g)
            def _():
                pltpu.make_async_copy(send3.at[g], buf3.at[g], rsem.at[T5]).start()

    start = lax.rem(g, 8)

    def first_two(t, _):
        statistics(lax.rem(start + t, 8))
        return 0

    def later(t, _):
        statistics(lax.rem(start + t, 8))
        send_t5(lax.rem(start + t - 1, 8))
        return 0

    def last_two(t, _):
        send_t5(lax.rem(start + t, 8))
        return 0

    lax.fori_loop(0, 2, first_two, 0)
    lax.fori_loop(2, 8, later, 0)
    lax.fori_loop(7, 9, last_two, 0)
    wait(rsem.at[T5], buf3)

    def depth(d):
        c0, c1 = buf3[2 * d, 0].astype(F32), buf3[2 * d + 1, 0].astype(F32)
        e0, e1 = buf3[2 * d, 1].astype(F32), buf3[2 * d + 1, 1].astype(F32)
        return (
            jnp.where(low_lane, c0, c1), jnp.where(low_lane, c1, c0), jnp.where(low_lane, e0, e1)
        )

    window = [None, depth(0), depth(1)]
    for d in range(16):
        present = [w for w in window if w is not None]
        less, imag, energy = [functools.reduce(jnp.add, terms) for terms in zip(*present)]
        real, imag = energy - less, pltpu.roll(imag, 64, 1)
        out[d] = 1.0 - jnp.sqrt(real * real + imag * imag) / (energy + 1e-6)
        window = window[1:] + [depth(d + 2) if d + 2 < 16 else None]

    wait(ssem.at[P0], ph1.at[0:15])
    wait(ssem.at[P1], ph2.at[0:15])
    for i in range(2):
        wait(ssem.at[T0 + i], buf1.at[i, 0:31])
        wait(ssem.at[T2 + i], buf1.at[i, 0:31])
        wait(ssem.at[T3 + i], send2.at[i, 0:31])
    wait(ssem.at[T5], buf3.at[0:31])


def local(volume, pupil_phase):
    wy, wyi, wx, tw = constant_tables()
    vm = pltpu.VMEM
    return pl.pallas_call(
        kernel,
        out_shape=jax.ShapeDtypeStruct((16, 16, 128), F32),
        in_specs=[pl.BlockSpec(memory_space=pltpu.HBM)] * 6,
        out_specs=pl.BlockSpec(memory_space=pltpu.VMEM),
        scratch_shapes=[
            vm((4, 256, 256), BF),
            vm((4, 256, 256), BF),
            vm((3, 256, 256), BF),
            vm((4, 16, 128), F32),
            vm((16, 16, 128), F32),
            vm((16, 16, 128), BF),
            vm((16, 16, 128), BF),
            vm((16, 16, 128), BF),
            vm((16, 16, 128), F32),
            vm((16, 16, 128), F32),
            vm((2, 2, 32, 16, 128), BF),
            vm((4, 256, 128), BF),
            vm((2, 32, 2, 16, 128), BF),
            vm((2, 32, 2, 16, 128), BF),
            vm((512, 256), F32),
            vm((512, 256), BF),
            vm((512, 256), F32),
            vm((2, 2, 16, 16, 128), F32),
            vm((2, 32, 3, 16, 128), BF),
            vm((2, 4, 3, 8, 16, 128), BF),
            vm((2, 4, 256, 256), F32),
            vm((3, 528, 128), F32),
            vm((32, 2, 16, 128), BF),
            vm((32, 2, 16, 128), BF),
            pltpu.SemaphoreType.DMA((9,)),
            pltpu.SemaphoreType.DMA((9,)),
            pltpu.SemaphoreType.DMA((5,)),
        ],
        compiler_params=pltpu.CompilerParams(
            collective_id=0, has_side_effects=True, vmem_limit_bytes=56 * 1024 * 1024
        ),
        name="decorrelation",
    )(
        volume.reshape(2, 4, 16, 16, 128),
        pupil_phase,
        jnp.asarray(wy),
        jnp.asarray(wyi),
        jnp.asarray(wx),
        jnp.asarray(tw),
    )


def solution(mesh):
    return jax.shard_map(
        local,
        mesh=mesh,
        in_specs=(P(None, None, "gy", "gx"), P(None, "gy", "gx")),
        out_specs=P(None, "gy", "gx"),
        check_vma=False,
    )
```

time: 103 us -> 87.2 us (0.85)
  Pallas kernels: 95.1 us -> 83.9 us
  local copies, waits for them, and re-layouts: 6.35 us -> 1.57 us
    pallas_call x1, Pallas kernels: 95.1 us -> 83.9 us  [local(): pl.pallas_call(kernel, out_shape=jax.ShapeDtypeStruct((16, 16, 128), F32)...]
    unnamed x13 -> x1, local copies, waits for them, and re-layouts: 6.35 us -> 1.57 us
where the time goes in v2:
time: 87.2 us; the launch traced here: 85.5 us
  Pallas kernels  83.9 us (96%)
  local copies, waits for them, and re-layouts  1.57 us (2%)
    pallas_call x1, Pallas kernels, local(): pl.pallas_call(kernel, out_shape=jax.ShapeDtypeStruct((16, 16, 128), F32)...  83.9 us

profile of v2, /device:TPU:1, one launch (start us, length us, event | category | flops | bytes accessed | tf_op | source)
XLA Modules:
  0.0 85.5 jit_solution(7074457915134097247)
XLA Ops:
  0.0 83.9 %decorrelation.1 = f32[16,16,128]{2,1,0:T(8,128)} custom-call(bf16[2,4,16,16,128]{4,3,2,1,0:T(8,128)(2,1)} %bitcast.1, f32[16,16,128]{2,1,0:T(8,128)} %pupil.1, bf16[4,256,256]{2,1,0:T(8,128)(2,1)} %constant.8.clone.wy_h, bf16[4,256,256]{2,1,0:T(8,128)(2,1)} %constant.9.clone.wyi_h, bf16[3,256,256]{2,1,0:T(8,128)(2,1)} %constant.10.clone.wx_h, ...), custom_call_target="tpu_custom_call" | custom-call | tf_op jit(solution)/shard_map/decorrelation/pallas_call | solution.py:414
  83.9 1.6 %copy.8 = f32[16,16,128]{2,1,0:T(8,128)} copy(f32[16,16,128]{2,1,0:T(8,128)} %decorrelation.1) | data formatting | bytes 262144

commit v3 on v2

--- a/solution.py
+++ b/solution.py
@@ -16,7 +16,7 @@
 GX = 16
 GY = 32
 P0, P1, T0, T2, T3, T5 = 0, 1, 2, 4, 6, 8
-EARLY = 16
+FIRST, SECOND = 16,31
 
 
 def stacked(matrix):
@@ -73,15 +73,19 @@
     return out
 
 
-def turn(i, count):
-    return lax.rem(i, 2) * ((i + 1) // 2) + (1 - lax.rem(i, 2)) * (count - i // 2)
+def around(i, step, count):
+    moved = i + step
+    return jnp.where(moved >= count, moved - count, moved)
+
+
+STEPS = [s for n in range(1, 8) for s in (n, 16 - n)] + [8]
 
 
 def kernel(
     vol, pupil, wy_h, wyi_h, wx_h, tw_h, out,
     wy, wyi, wx, tw, ph, ph0, ph1, ph2, cosine, sine,
     buf0, gy_s, send1, buf1, gx_s, cx_s, hx_s, fx_s, send2, buf2, hy_s, stats, send3, buf3,
-    ssem, rsem, csem,
+    ssem, rsem, csem, hand,
 ):
     a = lax.axis_index("gx")
     g = lax.axis_index("gy")
@@ -101,23 +105,19 @@
 
     barrier = pltpu.get_barrier_semaphore()
 
-    def greet_column(t, _):
-        pl.semaphore_signal(
-            barrier, inc=1, device_id=(a, lax.rem(g + t, GY)), device_id_type=MESH
-        )
-        return 0
-
-    def greet_plane(t, _):
-        peer = lax.rem(a + t, GX)
-        pl.semaphore_signal(barrier, inc=1, device_id=(peer, 2 * z), device_id_type=MESH)
-        pl.semaphore_signal(barrier, inc=1, device_id=(peer, 2 * z + 1), device_id_type=MESH)
-        return 0
-
-    lax.fori_loop(1, GY, greet_column, 0)
-    lax.fori_loop(1, GX, greet_plane, 0)
+    partner = 2 * z + 1 - h
+    corners = [a + (1 << b) * (1 - 2 * lax.rem(a // (1 << b), 2)) for b in range(4)]
+    greeted = [(a, 2 * around(z, s, 16) + h) for s in STEPS]
+    greeted += [(a, partner)] + [(c, g) for c in corners]
+    for device in greeted:
+        pl.semaphore_signal(barrier, inc=1, device_id=device, device_id_type=MESH)
     loads[0].wait()
     ph0[...] = ph[...].astype(BF)
-    pl.semaphore_wait(barrier, 61)
+    pl.semaphore_wait(barrier, 20)
+
+    def pass_on(n, device):
+        pl.semaphore_signal(hand.at[n], inc=1, device_id=device, device_id_type=MESH)
+        pl.semaphore_wait(hand.at[n], 1)
 
     def remote(src, dst, which, device):
         pltpu.make_async_remote_copy(
@@ -128,42 +128,38 @@
     def wait(sem, ref):
         pltpu.make_async_copy(ref, ref, sem).wait()
 
-    def send_p0(t, _):
-        zt = lax.rem(z + turn(t, 16), 16)
+    for step in STEPS:
+        zt = around(z, step, 16)
         remote(ph0.at[zt], ph1.at[z], P0, (a, 2 * zt + h))
-        return 0
-
-    lax.fori_loop(1, 16, send_p0, 0)
     pltpu.make_async_copy(ph0.at[z], ph1.at[z], rsem.at[P0]).start()
 
-    def send_t0(i, first, last):
-        def step(t, _):
-            gt = lax.rem(g + turn(t, GY), GY)
-            zt, ht = gt // 2, lax.rem(gt, 2)
-            remote(vol.at[:, 2 * ht + i, zt], buf0.at[i, :, g], T0 + i, (a, gt))
-            return 0
-
-        lax.fori_loop(first, last, step, 0)
+    order = [(s, False) for s in STEPS] + [(s, True) for s in STEPS + [0]]
+
+    def send_t0(i, peers):
+        for step, other in peers:
+            zt, ht = around(z, step, 16), 1 - h if other else h
+            remote(vol.at[:, 2 * ht + i, zt], buf0.at[i, :, g], T0 + i, (a, 2 * zt + ht))
 
     def keep_t0(i):
         pltpu.make_async_copy(
             vol.at[:, 2 * h + i, z], buf0.at[i, :, g], rsem.at[T0 + i]
         ).start()
 
-    send_t0(0, 1, GY)
+    send_t0(0, order[:15])
+    pass_on(0, (a, partner))
+    send_t0(0, order[15:])
     keep_t0(0)
+    send_t0(1, order[:FIRST])
     keep_t0(1)
+    for b in range(4):
+        pass_on(1 + b, (corners[b], g))
 
     wait(rsem.at[P0], ph1)
 
-    def send_p1(t, _):
-        at = lax.rem(a + turn(t, 16), 16)
+    for step in STEPS:
+        at = around(a, step, 16)
         remote(ph1.at[at], ph2.at[a], P1, (at, g))
-        return 0
-
-    lax.fori_loop(1, 16, send_p1, 0)
     pltpu.make_async_copy(ph1.at[a], ph2.at[a], rsem.at[P1]).start()
-    send_t0(1, 1, 1 + EARLY)
     for copy in loads[1:]:
         copy.wait()
     wait(rsem.at[P1], ph2)
@@ -195,12 +191,11 @@
             send1[i, 8 * k : 8 * k + 8, 1] = f[128:256].reshape(8, 16, 128)
 
     def send_t2(i):
-        def step(t, _):
-            jt = lax.rem(j + turn(t, 32), 32)
-            remote(send1.at[i, jt], buf1.at[i, j], T2 + i, (jt // 2, 2 * z + lax.rem(jt, 2)))
-            return 0
-
-        lax.fori_loop(1, 32, step, 0)
+        for step in STEPS + [0]:
+            at = around(a, step, 16)
+            for ht in (1 - h, h) if step else (1 - h,):
+                jt = 2 * at + ht
+                remote(send1.at[i, jt], buf1.at[i, j], T2 + i, (at, 2 * z + ht))
         pltpu.make_async_copy(send1.at[i, j], buf1.at[i, j], rsem.at[T2 + i]).start()
 
     def x_transforms(i):
@@ -252,7 +247,7 @@
             return jnp.where(low_lane, fx_s[1, c, n], fx_s[0, c, n])
 
         def pack(n):
-            before, after = lax.rem(n + 15, 16), lax.rem(n + 1, 16)
+            before, after = around(n, 15, 16), around(n, 1, 16)
             rims = []
             for c in range(2):
                 one, two = straight(n, c), crossed(n, c)
@@ -269,16 +264,11 @@
                     at_edge, rims[0][half], pltpu.roll(rims[1][half], 2, 1)
                 ).astype(BF)
 
-        def step(t, _):
-            n = lax.rem(a + turn(t, 16), 16)
+        for step in STEPS + [0]:
+            n = around(a, step, 16)
             pack(n)
-            for half in range(2):
-                remote(send2.at[i, 2 * n + half], place, T3 + i, (n, 2 * z + half))
-            return 0
-
-        lax.fori_loop(1, 16, step, 0)
-        pack(a)
-        remote(send2.at[i, 2 * a + 1 - h], place, T3 + i, (a, 2 * z + 1 - h))
+            for ht in (1 - h, h) if step else (1 - h,):
+                remote(send2.at[i, 2 * n + ht], place, T3 + i, (n, 2 * z + ht))
         pltpu.make_async_copy(send2.at[i, j], place, rsem.at[T3 + i]).start()
 
     def y_inverse(i):
@@ -294,10 +284,11 @@
     wait(rsem.at[T0], buf0.at[0])
     y_forward(0)
     send_t2(0)
-    send_t0(1, 1 + EARLY, GY)
+    send_t0(1, order[FIRST:SECOND])
     wait(rsem.at[T2], buf1.at[0])
     x_transforms(0)
     send_t3(0)
+    send_t0(1, order[SECOND:])
     wait(rsem.at[T0 + 1], buf0.at[1])
     y_forward(1)
     send_t2(1)
@@ -353,8 +344,11 @@
                 rows = stats[s, pl.ds(pl.multiple_of(128 * m + 16 * n, 8), 32), :]
                 sums.append(rows[7:23] + rows[8:24] + rows[9:25])
             gt = 8 * m + n
-            send3[gt, 0] = jnp.where(own, sums[0], pltpu.roll(sums[1], 64, 1)).astype(BF)
-            send3[gt, 1] = sums[2].astype(BF)
+            turned = pltpu.roll(sums[2], 64, 1)
+            first = jnp.where(h == 0, sums[2], turned)[0:8]
+            second = jnp.where(h == 0, turned, sums[2])[8:16]
+            send3[gt, 0:16] = jnp.where(own, sums[0], pltpu.roll(sums[1], 64, 1)).astype(BF)
+            send3[gt, 16:24] = jnp.where(low_lane[0:8], first, second).astype(BF)
 
             @pl.when(gt != g)
             def _():
@@ -385,10 +379,17 @@
     wait(rsem.at[T5], buf3)
 
     def depth(d):
-        c0, c1 = buf3[2 * d, 0].astype(F32), buf3[2 * d + 1, 0].astype(F32)
-        e0, e1 = buf3[2 * d, 1].astype(F32), buf3[2 * d + 1, 1].astype(F32)
+        both = [buf3[2 * d + n].astype(F32) for n in range(2)]
+        c0, c1 = both[0][0:16], both[1][0:16]
+        e0, e1 = both[0][16:24], both[1][16:24]
+        energy = [
+            jnp.where(low_lane[0:8], e0, pltpu.roll(e1, 64, 1)),
+            jnp.where(low_lane[0:8], pltpu.roll(e0, 64, 1), e1),
+        ]
         return (
-            jnp.where(low_lane, c0, c1), jnp.where(low_lane, c1, c0), jnp.where(low_lane, e0, e1)
+            jnp.where(low_lane, c0, c1),
+            jnp.where(low_lane, c1, c0),
+            jnp.concatenate(energy, axis=0),
         )
 
     window = [None, depth(0), depth(1)]
@@ -439,11 +440,12 @@
             vm((2, 4, 3, 8, 16, 128), BF),
             vm((2, 4, 256, 256), F32),
             vm((3, 528, 128), F32),
-            vm((32, 2, 16, 128), BF),
-            vm((32, 2, 16, 128), BF),
+            vm((32, 24, 128), BF),
+            vm((32, 24, 128), BF),
             pltpu.SemaphoreType.DMA((9,)),
             pltpu.SemaphoreType.DMA((9,)),
             pltpu.SemaphoreType.DMA((5,)),
+            pltpu.SemaphoreType.REGULAR((5,)),
         ],
         compiler_params=pltpu.CompilerParams(
             collective_id=0, has_side_effects=True, vmem_limit_bytes=56 * 1024 * 1024

time: 87.2 us -> 84.2 us (0.966)
  Pallas kernels: 83.9 us -> 81.7 us
    pallas_call x1, Pallas kernels: 83.9 us -> 81.7 us  [local(): pl.pallas_call(kernel, out_shape=jax.ShapeDtypeStruct((16, 16, 128), F32)...]
where the time goes in v3:
time: 84.2 us; the launch traced here: 83.3 us
  Pallas kernels  81.7 us (97%)
  local copies, waits for them, and re-layouts  1.57 us (2%)
    pallas_call x1, Pallas kernels, local(): pl.pallas_call(kernel, out_shape=jax.ShapeDtypeStruct((16, 16, 128), F32)...  81.7 us

profile of v3, /device:TPU:1, one launch (start us, length us, event | category | flops | bytes accessed | tf_op | source)
XLA Modules:
  0.0 83.3 jit_solution(9192964006302727333)
XLA Ops:
  0.0 81.7 %decorrelation.1 = f32[16,16,128]{2,1,0:T(8,128)} custom-call(bf16[2,4,16,16,128]{4,3,2,1,0:T(8,128)(2,1)} %bitcast.1, f32[16,16,128]{2,1,0:T(8,128)} %pupil.1, bf16[4,256,256]{2,1,0:T(8,128)(2,1)} %constant.8.clone.wy_h, bf16[4,256,256]{2,1,0:T(8,128)(2,1)} %constant.9.clone.wyi_h, bf16[3,256,256]{2,1,0:T(8,128)(2,1)} %constant.10.clone.wx_h, ...), custom_call_target="tpu_custom_call" | custom-call | tf_op jit(solution)/shard_map/decorrelation/pallas_call | solution.py:415
  81.7 1.6 %copy.8 = f32[16,16,128]{2,1,0:T(8,128)} copy(f32[16,16,128]{2,1,0:T(8,128)} %decorrelation.1) | data formatting | bytes 262144

commit v4 on v3

--- a/solution.py
+++ b/solution.py
@@ -78,7 +78,7 @@
     return jnp.where(moved >= count, moved - count, moved)
 
 
-STEPS = [s for n in range(1, 8) for s in (n, 16 - n)] + [8]
+STEPS = [8] + [s for n in range(7, 0, -1) for s in (n, 16 - n)]
 
 
 def kernel(

time: 84.2 us -> 80.9 us (0.961)
  Pallas kernels: 81.7 us -> 79.1 us
    pallas_call x1, Pallas kernels: 81.7 us -> 79.1 us  [local(): pl.pallas_call(kernel, out_shape=jax.ShapeDtypeStruct((16, 16, 128), F32)...]
where the time goes in v4:
time: 80.9 us; the launch traced here: 80.7 us
  Pallas kernels  79.1 us (98%)
  local copies, waits for them, and re-layouts  1.57 us (2%)
    pallas_call x1, Pallas kernels, local(): pl.pallas_call(kernel, out_shape=jax.ShapeDtypeStruct((16, 16, 128), F32)...  79.1 us

profile of v4, /device:TPU:1, one launch (start us, length us, event | category | flops | bytes accessed | tf_op | source)
XLA Modules:
  0.0 80.7 jit_solution(4748656698777836899)
XLA Ops:
  0.0 79.1 %decorrelation.1 = f32[16,16,128]{2,1,0:T(8,128)} custom-call(bf16[2,4,16,16,128]{4,3,2,1,0:T(8,128)(2,1)} %bitcast.1, f32[16,16,128]{2,1,0:T(8,128)} %pupil.1, bf16[4,256,256]{2,1,0:T(8,128)(2,1)} %constant.8.clone.wy_h, bf16[4,256,256]{2,1,0:T(8,128)(2,1)} %constant.9.clone.wyi_h, bf16[3,256,256]{2,1,0:T(8,128)(2,1)} %constant.10.clone.wx_h, ...), custom_call_target="tpu_custom_call" | custom-call | tf_op jit(solution)/shard_map/decorrelation/pallas_call | solution.py:415
  79.2 1.6 %copy.8 = f32[16,16,128]{2,1,0:T(8,128)} copy(f32[16,16,128]{2,1,0:T(8,128)} %decorrelation.1) | data formatting | bytes 262144

commit v5 on v4

--- a/solution.py
+++ b/solution.py
@@ -149,7 +149,6 @@
     pass_on(0, (a, partner))
     send_t0(0, order[15:])
     keep_t0(0)
-    send_t0(1, order[:FIRST])
     keep_t0(1)
     for b in range(4):
         pass_on(1 + b, (corners[b], g))
@@ -160,17 +159,15 @@
         at = around(a, step, 16)
         remote(ph1.at[at], ph2.at[a], P1, (at, g))
     pltpu.make_async_copy(ph1.at[a], ph2.at[a], rsem.at[P1]).start()
+    send_t0(1, order[:FIRST])
     for copy in loads[1:]:
         copy.wait()
-    wait(rsem.at[P1], ph2)
 
     def angles(k, _):
         phase = ph2[k].astype(F32)
         cosine[k] = jnp.cos(phase)
         sine[k] = jnp.sin(phase)
         return 0
-
-    lax.fori_loop(0, 16, angles, 0)
 
     def y_forward(i):
         def columns(n, _):
@@ -285,6 +282,8 @@
     y_forward(0)
     send_t2(0)
     send_t0(1, order[FIRST:SECOND])
+    wait(rsem.at[P1], ph2)
+    lax.fori_loop(0, 16, angles, 0)
     wait(rsem.at[T2], buf1.at[0])
     x_transforms(0)
     send_t3(0)
@@ -337,8 +336,11 @@
                 value = value + pltpu.roll(value, 1, 1) + pltpu.roll(value, 127, 1)
                 stats[s, pl.ds(pl.multiple_of(8 + 128 * m + row, 8), 16), :] = value
 
-    def send_t5(n):
-        for m in range(4):
+    FAR, NEAR = (2, 1, 3), (0,)
+
+    def send_t5(n, offsets):
+        for offset in offsets:
+            m = around(z // 4, offset, 4) if offset else z // 4
             sums = []
             for s in range(3):
                 rows = stats[s, pl.ds(pl.multiple_of(128 * m + 16 * n, 8), 32), :]
@@ -366,16 +368,21 @@
 
     def later(t, _):
         statistics(lax.rem(start + t, 8))
-        send_t5(lax.rem(start + t - 1, 8))
+        send_t5(lax.rem(start + t - 1, 8), FAR)
         return 0
 
     def last_two(t, _):
-        send_t5(lax.rem(start + t, 8))
+        send_t5(lax.rem(start + t, 8), FAR)
+        return 0
+
+    def near_ones(t, _):
+        send_t5(lax.rem(start + t, 8), NEAR)
         return 0
 
     lax.fori_loop(0, 2, first_two, 0)
     lax.fori_loop(2, 8, later, 0)
     lax.fori_loop(7, 9, last_two, 0)
+    lax.fori_loop(1, 9, near_ones, 0)
     wait(rsem.at[T5], buf3)
 
     def depth(d):

time: 80.9 us -> 79.1 us (0.978)
  Pallas kernels: 79.1 us -> 76.7 us
    pallas_call x1, Pallas kernels: 79.1 us -> 76.7 us  [local(): pl.pallas_call(kernel, out_shape=jax.ShapeDtypeStruct((16, 16, 128), F32)...]
where the time goes in v5:
time: 79.1 us; the launch traced here: 78.3 us
  Pallas kernels  76.7 us (97%)
  local copies, waits for them, and re-layouts  1.57 us (2%)
    pallas_call x1, Pallas kernels, local(): pl.pallas_call(kernel, out_shape=jax.ShapeDtypeStruct((16, 16, 128), F32)...  76.7 us

profile of v5, /device:TPU:1, one launch (start us, length us, event | category | flops | bytes accessed | tf_op | source)
XLA Modules:
  0.0 78.3 jit_solution(18440245257771693911)
XLA Ops:
  0.0 76.7 %decorrelation.1 = f32[16,16,128]{2,1,0:T(8,128)} custom-call(bf16[2,4,16,16,128]{4,3,2,1,0:T(8,128)(2,1)} %bitcast.1, f32[16,16,128]{2,1,0:T(8,128)} %pupil.1, bf16[4,256,256]{2,1,0:T(8,128)(2,1)} %constant.8.clone.wy_h, bf16[4,256,256]{2,1,0:T(8,128)(2,1)} %constant.9.clone.wyi_h, bf16[3,256,256]{2,1,0:T(8,128)(2,1)} %constant.10.clone.wx_h, ...), custom_call_target="tpu_custom_call" | custom-call | tf_op jit(solution)/shard_map/decorrelation/pallas_call | solution.py:422
  76.7 1.6 %copy.8 = f32[16,16,128]{2,1,0:T(8,128)} copy(f32[16,16,128]{2,1,0:T(8,128)} %decorrelation.1) | data formatting | bytes 262144

commit v6 on v5

--- a/solution.py
+++ b/solution.py
@@ -85,7 +85,7 @@
     vol, pupil, wy_h, wyi_h, wx_h, tw_h, out,
     wy, wyi, wx, tw, ph, ph0, ph1, ph2, cosine, sine,
     buf0, gy_s, send1, buf1, gx_s, cx_s, hx_s, fx_s, send2, buf2, hy_s, stats, send3, buf3,
-    ssem, rsem, csem, hand,
+    ssem, rsem, csem, hand, result,
 ):
     a = lax.axis_index("gx")
     g = lax.axis_index("gy")
@@ -291,11 +291,11 @@
     wait(rsem.at[T0 + 1], buf0.at[1])
     y_forward(1)
     send_t2(1)
-    wait(rsem.at[T3], buf2.at[0])
-    y_inverse(0)
     wait(rsem.at[T2 + 1], buf1.at[1])
     x_transforms(1)
     send_t3(1)
+    wait(rsem.at[T3], buf2.at[0])
+    y_inverse(0)
     wait(rsem.at[T3 + 1], buf2.at[1])
     y_inverse(1)
 
@@ -399,13 +399,20 @@
             jnp.concatenate(energy, axis=0),
         )
 
+    stores = []
     window = [None, depth(0), depth(1)]
     for d in range(16):
         present = [w for w in window if w is not None]
         less, imag, energy = [functools.reduce(jnp.add, terms) for terms in zip(*present)]
         real, imag = energy - less, pltpu.roll(imag, 64, 1)
-        out[d] = 1.0 - jnp.sqrt(real * real + imag * imag) / (energy + 1e-6)
+        result[d] = 1.0 - jnp.sqrt(real * real + imag * imag) / (energy + 1e-6)
         window = window[1:] + [depth(d + 2) if d + 2 < 16 else None]
+        if d % 4 == 3:
+            rows = pl.ds(d - 3, 4)
+            stores.append(
+                pltpu.make_async_copy(result.at[rows], out.at[rows], csem.at[5 + d // 4])
+            )
+            stores[-1].start()
 
     wait(ssem.at[P0], ph1.at[0:15])
     wait(ssem.at[P1], ph2.at[0:15])
@@ -414,6 +421,8 @@
         wait(ssem.at[T2 + i], buf1.at[i, 0:31])
         wait(ssem.at[T3 + i], send2.at[i, 0:31])
     wait(ssem.at[T5], buf3.at[0:31])
+    for store in stores:
+        store.wait()
 
 
 def local(volume, pupil_phase):
@@ -423,7 +432,7 @@
         kernel,
         out_shape=jax.ShapeDtypeStruct((16, 16, 128), F32),
         in_specs=[pl.BlockSpec(memory_space=pltpu.HBM)] * 6,
-        out_specs=pl.BlockSpec(memory_space=pltpu.VMEM),
+        out_specs=pl.BlockSpec(memory_space=pltpu.HBM),
         scratch_shapes=[
             vm((4, 256, 256), BF),
             vm((4, 256, 256), BF),
@@ -451,8 +460,9 @@
             vm((32, 24, 128), BF),
             pltpu.SemaphoreType.DMA((9,)),
             pltpu.SemaphoreType.DMA((9,)),
-            pltpu.SemaphoreType.DMA((5,)),
+            pltpu.SemaphoreType.DMA((9,)),
             pltpu.SemaphoreType.REGULAR((5,)),
+            vm((16, 16, 128), F32),
         ],
         compiler_params=pltpu.CompilerParams(
             collective_id=0, has_side_effects=True, vmem_limit_bytes=56 * 1024 * 1024

time: 79.1 us -> 79.1 us (level)
  no operation moved by 1% of the time
where the time goes in v6:
time: 79.1 us; the launch traced here: 78.3 us
  Pallas kernels  76.7 us (97%)
  local copies, waits for them, and re-layouts  1.57 us (2%)
    pallas_call x1, Pallas kernels, local(): pl.pallas_call(kernel, out_shape=jax.ShapeDtypeStruct((16, 16, 128), F32)...  76.7 us

profile of v6, /device:TPU:1, one launch (start us, length us, event | category | flops | bytes accessed | tf_op | source)
XLA Modules:
  0.0 78.3 jit_solution(18237431374155368333)
XLA Ops:
  0.0 76.7 %decorrelation.1 = f32[16,16,128]{2,1,0:T(8,128)} custom-call(bf16[2,4,16,16,128]{4,3,2,1,0:T(8,128)(2,1)} %bitcast.1, f32[16,16,128]{2,1,0:T(8,128)} %pupil.1, bf16[4,256,256]{2,1,0:T(8,128)(2,1)} %constant.8.clone.wy_h, bf16[4,256,256]{2,1,0:T(8,128)(2,1)} %constant.9.clone.wyi_h, bf16[3,256,256]{2,1,0:T(8,128)(2,1)} %constant.10.clone.wx_h, ...), custom_call_target="tpu_custom_call" | custom-call | tf_op jit(solution)/shard_map/decorrelation/pallas_call | solution.py:431
  76.7 1.6 %copy.8 = f32[16,16,128]{2,1,0:T(8,128)} copy(f32[16,16,128]{2,1,0:T(8,128)} %decorrelation.1) | data formatting | bytes 262144
